TPU v7x, 32 devices: a whole 2x2x4 slice. The times are simulated.
32 devices in a mesh: ep: 4 (over y, core), tp: 8 (over z, x).
Axes of the slice: x: 2, y: 2, z: 4, core: 2. Of those that a mesh axis runs over, the one named last changes fastest.
Arguments:
- query_key_value: bfloat16 [16, 256, 3, 1792], P('ep', 'tp'), may hold values from -6 to 6
- residual: bfloat16 [16, 256, 1792], P('ep', 'tp'), may hold values from -6 to 6
- norm_gain: float32 [1792], replicated, may hold values from 0.1 to 1.9
- expert_ids: int32 [16, 256, 2], P('ep', 'tp'), may hold values from 0 to 7, as said below
- route_gates: float32 [16, 256, 2], P('ep', 'tp'), may hold values from 0.2 to 1
- slot_index: int32 [16, 256, 2], P('ep', 'tp'), may hold values from -1 to 31, as said below
- w_gate: bfloat16 [8, 1792, 7168], P('ep', None, 'tp'), may hold values from -0.125 to 0.125
- w_up: bfloat16 [8, 1792, 7168], P('ep', None, 'tp'), may hold values from -0.125 to 0.125
- w_down: bfloat16 [8, 7168, 1792], P('ep', 'tp'), may hold values from -0.0625 to 0.0625
Outputs:
- block_out: bfloat16 [16, 256, 1792], P('ep', 'tp')
Inputs may be any that keep to these rules, and one draw needn't show every extreme that they name: `expert_ids`: each token names two different experts. One expert is the first choice of 32 or more tokens of every device (a device holds 4 frames by 32 sites). `slot_index`: the rank of an assignment among the assignments of the same expert on the same device, counted in the order frame, site, choice; -1 where that rank is 32 or more. Every device fills all 32 slots of some expert.
All inputs are finite; a program needn't handle non-finite values.
Results may differ from a plain program's by a relative error of at most 0.0095.
Values may be sent and summed in bfloat16 or wider, within the bound.
A program may use at most 128 MiB of HBM per device.

v0:
```python
import math

import jax
import jax.numpy as jnp
from jax import lax
from jax.sharding import PartitionSpec as P

HD = 64


def attend(query_part, key_part, value_part):
    frames_q, site_count, model_width = query_part.shape
    frames_k = key_part.shape[0]
    head_count = model_width // HD
    query_h = query_part.reshape(frames_q, site_count, head_count, HD)
    key_h = key_part.reshape(frames_k, site_count, head_count, HD)
    value_h = value_part.reshape(frames_k, site_count, head_count, HD)
    scores = jnp.einsum(
        "fshd,gshd->shfg", query_h, key_h, preferred_element_type=jnp.float32
    ) / math.sqrt(HD)
    scores = scores - jnp.max(scores, axis=-1, keepdims=True)
    expo = jnp.exp(scores)
    probs = (expo / jnp.sum(expo, axis=-1, keepdims=True)).astype(jnp.bfloat16)
    mixed = jnp.einsum("shfg,gshd->fshd", probs, value_h, preferred_element_type=jnp.float32)
    return mixed.reshape(frames_q, site_count, model_width).astype(jnp.bfloat16)


def body(
    query_key_value, residual, norm_gain, expert_ids, route_gates, slot_index, w_gate, w_up, w_down
):
    frames_local = residual.shape[0]
    sites_local = residual.shape[1]
    model_width = residual.shape[2]
    groups = lax.axis_size("ep")
    split_view = query_key_value.reshape(
        frames_local, groups, sites_local // groups, 3, model_width
    )
    site_block = lax.all_to_all(split_view, "ep", split_axis=1, concat_axis=0, tiled=True)
    by_sites = attend(site_block[:, 0, :, 0], site_block[:, 0, :, 1], site_block[:, 0, :, 2])[
        :, None
    ]
    attended = lax.all_to_all(by_sites, "ep", split_axis=0, concat_axis=1, tiled=True).reshape(
        frames_local, sites_local, model_width
    )
    tokens = frames_local * sites_local
    hidden = (residual.astype(jnp.float32) + attended.astype(jnp.float32)).reshape(
        tokens, model_width
    )
    scale = lax.rsqrt(jnp.mean(hidden * hidden, axis=-1, keepdims=True) + 1e-06)
    normed = (hidden * scale * norm_gain).astype(jnp.bfloat16)
    experts_local = w_gate.shape[0]
    experts_all = experts_local * groups
    capacity = 2 * tokens // experts_all
    chosen = expert_ids.reshape(tokens, 2)
    slots = slot_index.reshape(tokens, 2)
    gates = route_gates.reshape(tokens, 2)
    valid = slots >= 0
    slot_target = jnp.where(valid, slots, capacity)
    spread_rows = jnp.broadcast_to(normed[:, None, :], (tokens, 2, model_width))
    outgoing = (
        jnp.zeros((capacity, experts_all, model_width), jnp.bfloat16)
        .at[slot_target, chosen]
        .set(spread_rows, mode="drop")
    )
    arrived = lax.all_to_all(outgoing, "ep", split_axis=1, concat_axis=0, tiled=True)
    gathered = lax.all_gather(arrived, "tp", axis=0, tiled=True)
    gate_val = jnp.einsum("red,edf->ref", gathered, w_gate, preferred_element_type=jnp.float32)
    up_val = jnp.einsum("red,edf->ref", gathered, w_up, preferred_element_type=jnp.float32)
    active = (jax.nn.silu(gate_val) * up_val).astype(jnp.bfloat16)
    summed = lax.psum_scatter(
        jnp.einsum("ref,efd->red", active, w_down, preferred_element_type=jnp.float32).astype(
            jnp.bfloat16
        ),
        "tp",
        scatter_dimension=0,
        tiled=True,
    )
    returned = lax.all_to_all(summed, "ep", split_axis=0, concat_axis=1, tiled=True)
    picked = returned[jnp.where(valid, slots, 0), chosen]
    weights = jnp.where(valid, gates, 0.0)
    combined = hidden + jnp.sum(weights[:, :, None] * picked.astype(jnp.float32), axis=1)
    return combined.reshape(frames_local, sites_local, model_width).astype(jnp.bfloat16)


def solution(mesh):
    return jax.shard_map(
        body,
        mesh=mesh,
        in_specs=(
            P("ep", "tp", None, None),
            P("ep", "tp", None),
            P(),
            P("ep", "tp", None),
            P("ep", "tp", None),
            P("ep", "tp", None),
            P("ep", None, "tp"),
            P("ep", None, "tp"),
            P("ep", "tp", None),
        ),
        out_specs=P("ep", "tp", None),
        check_vma=False,
    )
```

profile of v0, /device:TPU:13, one launch (start us, length us, event | category | flops | bytes accessed | tf_op | source)
XLA Modules:
  0.0 406.1 jit_solution(8762418548985358138)
XLA Ops:
  6.5 1.4 copy.41
  8.0 19.2 %all_to_all.63 = bf16[4,4,8,3,1792]{4,2,3,0,1:T(8,128)(2,1)S(1)} all-to-all(bf16[4,4,8,3,1792]{4,2,3,0,1:T(8,128)(2,1)S(1)} %copy.41), channel_id=1, replica_groups=mesh['ep'=4,'tp'=8] {'ep'}, dimensions={1} | all-to-all | bytes 2752512 | tf_op jit(solution)/shard_map/all_to_all | solution.py:38
  27.2 0.1 fusion.33
  27.3 1.0 reshape_squeeze.10
  28.3 1.0 reshape_squeeze.9
  29.3 2.0 reshape_squeeze.11
  31.3 2.9 fusion.34
  34.2 0.0 copy-start.1
  34.2 0.0 copy-start.4
  34.2 0.0 copy-start
  34.2 0.0 copy-start.2
  34.2 2.6 fusion.6
  36.8 0.3 copy.46
  37.1 1.6 convert_element_type.60
  38.7 5.6 %all-to-all-start.1 = ((bf16[16,1,8,1792]{3,2,1,0:T(8,128)(2,1)}), bf16[16,1,8,1792]{3,2,1,0:T(8,128)(2,1)S(1)}, u32[]{:S(2)}, u32[]{:S(2)}) async-start(bf16[16,1,8,1792]{3,2,1,0:T(8,128)(2,1)} %bitcast.7), calls=%async_computation.1 | async-start | bytes 917504 | tf_op jit(solution)/shard_map/all_to_all | solution.py:42
  44.3 0.0 all-gather.2.cloned.1.call-start
  44.3 0.0 copy-done.1
  44.3 0.1 reshape.172
  44.4 0.0 copy-done.4
  44.4 0.1 reshape.173
  44.5 0.1 copy.54
  44.6 0.1 reshape.183
  44.7 5.8 %all-to-all-done.1 = bf16[16,1,8,1792]{3,2,1,0:T(8,128)(2,1)S(1)} async-done(((bf16[16,1,8,1792]{3,2,1,0:T(8,128)(2,1)}), bf16[16,1,8,1792]{3,2,1,0:T(8,128)(2,1)S(1)}, u32[]{:S(2)}, u32[]{:S(2)}) %all-to-all-start.1) | async-done | bytes 458784 | tf_op jit(solution)/shard_map/all_to_all | solution.py:42
  50.5 0.0 copy-done
  50.5 0.2 multiply_reduce_fusion.2
  50.8 0.1 rsqrt.12
  50.8 0.0 copy-done.2
  50.8 0.1 fusion.8
  51.0 0.5 broadcast_in_dim.15
  51.5 0.3 reshape.185
  51.8 0.1 broadcast_in_dim.13
  51.9 20.9 %scatter_fusion = bf16[32,8,1792]{2,1,0:T(8,128)(2,1)S(1)} fusion(bf16[32,8,1792]{2,1,0:T(8,128)(2,1)S(1)} %broadcast_in_dim.13, s32[256]{0:T(256)S(1)} %reshape.183, bf16[256,1792]{1,0:T(8,128)(2,1)S(1)} %reshape.185), kind=kCustom, calls=%fused_computation.1 | custom fusion | bytes 2754560 | tf_op jit(solution)/shard_map/scatter | solution.py:63
  72.8 0.2 copy.55
  73.0 15.5 %all_to_all.64 = bf16[32,8,1792]{2,0,1:T(8,128)(2,1)S(1)} all-to-all(bf16[32,8,1792]{2,0,1:T(8,128)(2,1)S(1)} %copy.55), channel_id=1, replica_groups=mesh['ep'=4,'tp'=8] {'ep'}, dimensions={1} | all-to-all | bytes 1835008 | tf_op jit(solution)/shard_map/all_to_all | solution.py:65
  88.5 1.0 copy.56
  89.4 0.0 all-gather.2.cloned.1.call-update
  89.5 0.2 reduce-scatter.2.cloned.1.call-start
  89.7 110.9 %all-gather.2.cloned.1.call-done = bf16[1024,2,1792]{2,0,1:T(8,128)(2,1)} async-done(((bf16[128,2,1792]{2,0,1:T(8,128)(2,1)}), bf16[1024,2,1792]{2,0,1:T(8,128)(2,1)}) %all-gather.2.cloned.1.call-update) | async-done | bytes 7340048 | tf_op jit(solution)/shard_map/all_gather | solution.py:66
  200.6 13.7 %fusion.39 = f32[2,1024,896]{2,1,0:T(8,128)} fusion(bf16[1024,2,1792]{2,0,1:T(8,128)(2,1)} %all-gather.2.cloned.1.call-done, bf16[2,1792,896]{2,1,0:T(8,128)(2,1)} %param.16), kind=kOutput, calls=%fused_computation.50 | convolution fusion | flops 6576668672 | bytes 21102592 | tf_op jit(solution)/shard_map/red,edf->ref/dot_general | solution.py:68
  214.3 22.7 %convert_bitcast_fusion = bf16[1024,2,1792]{2,0,1:T(8,128)(2,1)} fusion(bf16[2,896,1792]{2,1,0:T(8,128)(2,1)} %param.17, f32[2,1024,896]{2,1,0:T(8,128)} %fusion.39, bf16[1024,2,1792]{2,0,1:T(8,128)(2,1)} %all-gather.2.cloned.1.call-done, bf16[2,1792,896]{2,1,0:T(8,128)(2,1)} %param.15), kind=kOutput, calls=%fused_computation.10 | convolution fusion | flops 13168017408 | bytes 34865152 | tf_op jit(solution)/shard_map/ref,efd->red/dot_general | solution.py:71
  237.0 0.0 copy-start.3
  237.0 0.0 reduce-scatter.2.cloned.1.call-update
  237.0 132.1 %reduce-scatter.2.cloned.1.call-done = bf16[128,2,1792]{2,0,1:T(8,128)(2,1)} async-done(((bf16[1024,2,1792]{2,0,1:T(8,128)(2,1)}), bf16[128,2,1792]{2,0,1:T(8,128)(2,1)}) %reduce-scatter.2.cloned.1.call-update) | async-done | bytes 917520 | tf_op jit(solution)/shard_map/reduce_scatter | solution.py:70
  369.1 3.1 copy.57
  372.2 4.5 %all-to-all-start.3 = ((bf16[128,2,1792]{2,1,0:T(2,128)(2,1)}), bf16[128,2,1792]{2,1,0:T(2,128)(2,1)S(1)}, u32[]{:S(2)}, u32[]{:S(2)}) async-start(bf16[128,2,1792]{2,1,0:T(2,128)(2,1)} %copy.57), calls=%async_computation.4 | async-start | bytes 1835008 | tf_op jit(solution)/shard_map/all_to_all | solution.py:78
  376.7 0.1 copy.59
  376.8 0.1 reshape.177
  377.0 0.0 copy-done.3
  377.0 0.1 copy.61
  377.1 10.6 %all-to-all-done.3 = bf16[128,2,1792]{2,1,0:T(2,128)(2,1)S(1)} async-done(((bf16[128,2,1792]{2,1,0:T(2,128)(2,1)}), bf16[128,2,1792]{2,1,0:T(2,128)(2,1)S(1)}, u32[]{:S(2)}, u32[]{:S(2)}) %all-to-all-start.3) | async-done | bytes 917536 | tf_op jit(solution)/shard_map/all_to_all | solution.py:78
  387.8 0.6 copy.88
  388.4 0.3 all_to_all.58
  388.7 4.7 %gather_fusion = bf16[256,1792]{1,0:T(8,128)(2,1)} fusion(bf16[32,8,1792]{2,1,0:T(8,128)(2,1)S(1)} %all_to_all.58, s32[256]{0:T(256)S(1)} %reshape.177), kind=kCustom, calls=%fused_computation | custom fusion | bytes 1837056 | tf_op jit(solution)/shard_map/gather | solution.py:79
  393.5 2.3 reshape.189
  395.8 2.6 multiply_reduce_fusion
  398.4 0.9 add_convert_fusion
  (5 shorter events, 0.0 us)
Async XLA Ops:
  34.2 10.1 %copy-start.1 = (s32[4,32,2]{1,2,0:T(2,128)S(1)}, s32[4,32,2]{1,2,0:T(2,128)}, u32[]{:S(2)}) copy-start(s32[4,32,2]{1,2,0:T(2,128)} %param.14) | copy-start | bytes 3076
  34.2 10.1 %copy-start.4 = (s32[4,32,2]{1,2,0:T(2,128)S(1)}, s32[4,32,2]{1,2,0:T(2,128)}, u32[]{:S(2)}) copy-start(s32[4,32,2]{1,2,0:T(2,128)} %param.12) | copy-start | bytes 3076
  34.2 16.3 %copy-start = (bf16[4,32,1792]{2,1,0:T(8,128)(2,1)S(1)}, bf16[4,32,1792]{2,1,0:T(8,128)(2,1)}, u32[]{:S(2)}) copy-start(bf16[4,32,1792]{2,1,0:T(8,128)(2,1)} %param.10) | copy-start | bytes 1376260
  34.2 16.6 %copy-start.2 = (f32[1792]{0:T(1024)S(1)}, f32[1792]{0:T(1024)}, u32[]{:S(2)}) copy-start(f32[1792]{0:T(1024)} %param.11) | copy-start | bytes 21508
  38.7 11.8 %all-to-all-start.1 = ((bf16[16,1,8,1792]{3,2,1,0:T(8,128)(2,1)}), bf16[16,1,8,1792]{3,2,1,0:T(8,128)(2,1)S(1)}, u32[]{:S(2)}, u32[]{:S(2)}) async-start(bf16[16,1,8,1792]{3,2,1,0:T(8,128)(2,1)} %bitcast.7), calls=%async_computation.1 | async-start | bytes 917504 | tf_op jit(solution)/shard_map/all_to_all | solution.py:42
  44.3 156.3 %all-gather.2.cloned.1.call-start = ((), (), s32[]{:S(2)}) async-start(), calls=%async_computation.5 | async-start | bytes 8257536 | tf_op jit(solution)/shard_map/all_gather | solution.py:66
  89.5 279.7 %reduce-scatter.2.cloned.1.call-start = ((), (), s32[]{:S(2)}) async-start(), calls=%async_computation.6 | async-start | bytes 8257536 | tf_op jit(solution)/shard_map/reduce_scatter | solution.py:70
  237.0 140.0 %copy-start.3 = (f32[4,32,2]{1,2,0:T(2,128)S(1)}, f32[4,32,2]{1,2,0:T(2,128)}, u32[]{:S(2)}) copy-start(f32[4,32,2]{1,2,0:T(2,128)} %param.13) | copy-start | bytes 3076
  372.2 15.5 %all-to-all-start.3 = ((bf16[128,2,1792]{2,1,0:T(2,128)(2,1)}), bf16[128,2,1792]{2,1,0:T(2,128)(2,1)S(1)}, u32[]{:S(2)}, u32[]{:S(2)}) async-start(bf16[128,2,1792]{2,1,0:T(2,128)(2,1)} %copy.57), calls=%async_computation.4 | async-start | bytes 1835008 | tf_op jit(solution)/shard_map/all_to_all | solution.py:78
Sparse Core Ops, SparseCore 0:
  89.6 110.9 all-gather.1
  237.1 131.9 reduce-scatter.1
where the time goes:
time: 410 us; the launch traced here: 406 us
  waiting for transfers between devices  260 us (63%)
  local copies, waits for them, and re-layouts  42.3 us (10%)
  matrix products  41.9 us (10%)
  blocking collectives  34.7 us (8%)
  between operations  13.6 us (3%)
  starting transfers between devices  10.3 us (3%)
    reduce_scatter x1, waiting for transfers between devices, body(): lax.psum_scatter(jnp.einsum('ref,efd->red', active, w_down, preferred_ele...  132 us
    all_gather x1, waiting for transfers between devices, body(): gathered = lax.all_gather(arrived, 'tp', axis=0, tiled=True)  111 us
    dot_general x1, matrix products, body(): jnp.einsum('ref,efd->red', active, w_down, preferred_element_type=jnp.flo...  22.7 us
    scatter x2, local copies, waits for them, and re-layouts, body(): outgoing = jnp.zeros((capacity, experts_all, model_width), jnp.bfloat16)....  21.1 us
    all_to_all x1, blocking collectives, body(): lax.all_to_all(split_view, 'ep', split_axis=1, concat_axis=0, tiled=True)  19.2 us
    all_to_all x1, blocking collectives, body(): lax.all_to_all(outgoing, 'ep', split_axis=1, concat_axis=0, tiled=True)  15.5 us
    dot_general x1, matrix products, body(): jnp.einsum('red,edf->ref', gathered, w_up, preferred_element_type=jnp.flo...  13.7 us
    all_to_all x1, waiting for transfers between devices, body(): lax.all_to_all(summed, 'ep', split_axis=0, concat_axis=1, tiled=True)  10.6 us
  transfers between devices with their start and end apart: 4, of which 4 were waited for; matrix products, arithmetic and copies ran while one was open for 0% of the time, Pallas kernels for 0%

commit v1 on v0

--- a/solution.py
+++ b/solution.py
@@ -1,11 +1,338 @@
+import functools
 import math
 
 import jax
 import jax.numpy as jnp
 from jax import lax
+from jax.experimental import pallas as pl
+from jax.experimental.pallas import tpu as pltpu
 from jax.sharding import PartitionSpec as P
 
 HD = 64
+COLUMNS = 2
+VMEM_BYTES = 58 * 1024 * 1024
+MESH = pl.DeviceIdType.MESH
+
+
+def near_first(depth):
+    return [sorted(range(depth), key=lambda other: (abs(other - at), other)) for at in range(depth)]
+
+
+def lookup(table, row, column):
+    total = 0
+    for i, values in enumerate(table):
+        for j, value in enumerate(values):
+            if value:
+                total = total + jnp.where(jnp.logical_and(row == i, column == j), value, 0)
+    return total
+
+
+def expert_kernel(
+    groups, depth, capacity, out_ref, wg_hbm, wu_hbm, wd_hbm, back_ref,
+    wg, wu, wd, rows, part, from_x, from_z, back,
+    w_sem, disp_send, ag_send, ag_recv, x_send, x_recv, z_send, z_recv, back_send, back_recv,
+):
+    me_e = lax.axis_index("ep")
+    me_t = lax.axis_index("tp")
+    z = me_t // COLUMNS
+    x = me_t % COLUMNS
+    partner = z * COLUMNS + (1 - x)
+    above = me_t + COLUMNS
+    below = me_t - COLUMNS
+    has_above = z < depth - 1
+    has_below = z > 0
+    experts = wg.shape[0]
+    width = rows.shape[-1]
+    order = near_first(depth)
+
+    weight_copies = [
+        pltpu.make_async_copy(src, dst, w_sem.at[i])
+        for i, (src, dst) in enumerate(((wg_hbm, wg), (wu_hbm, wu), (wd_hbm, wd)))
+    ]
+    for copy in weight_copies:
+        copy.start()
+
+    barrier = pltpu.get_barrier_semaphore()
+    for i in range(1, groups):
+        pl.semaphore_signal(
+            barrier, inc=1, device_id=(lax.rem(me_e + i, groups), me_t), device_id_type=MESH
+        )
+    pl.semaphore_signal(barrier, inc=1, device_id=(me_e, partner), device_id_type=MESH)
+
+    @pl.when(has_above)
+    def _():
+        pl.semaphore_signal(barrier, inc=1, device_id=(me_e, above), device_id_type=MESH)
+
+    @pl.when(has_below)
+    def _():
+        pl.semaphore_signal(barrier, inc=1, device_id=(me_e, below), device_id_type=MESH)
+
+    peers = groups + jnp.where(has_above, 1, 0) + jnp.where(has_below, 1, 0)
+    pl.semaphore_wait(barrier, peers)
+
+    def remote(src, dst, send, recv, device):
+        return pltpu.make_async_remote_copy(
+            src_ref=src, dst_ref=dst, send_sem=send, recv_sem=recv,
+            device_id=device, device_id_type=MESH,
+        )
+
+    def dispatch(to_e):
+        return remote(
+            out_ref.at[to_e], rows.at[me_t, me_e], disp_send.at[to_e], ag_recv.at[me_t, me_e],
+            (to_e, me_t),
+        )
+
+    def gather(way, zt, c, to_t):
+        block = rows.at[zt * COLUMNS + x, c]
+        return remote(
+            block, block, ag_send.at[way, zt, c], ag_recv.at[zt * COLUMNS + x, c], (me_e, to_t)
+        )
+
+    def arrival(t, c):
+        block = rows.at[t, c]
+        return remote(block, block, ag_send.at[0, 0, 0], ag_recv.at[t, c], (me_e, partner))
+
+    def x_sum(zt, c):
+        return remote(
+            part.at[zt * COLUMNS + (1 - x), c], from_x.at[zt, c], x_send.at[zt, c],
+            x_recv.at[zt, c], (me_e, partner),
+        )
+
+    def z_sum(way, zt, c, to_t):
+        return remote(
+            part.at[zt * COLUMNS + x, c], from_z.at[way, zt, c], z_send.at[zt, c],
+            z_recv.at[way, zt, c], (me_e, to_t),
+        )
+
+    def send_back(c):
+        return remote(
+            part.at[me_t, c], back.at[me_e], back_send.at[c], back_recv.at[me_e], (c, me_t)
+        )
+
+    def back_arrival(c):
+        return remote(part.at[me_t, c], back.at[c], back_send.at[c], back_recv.at[c], (c, me_t))
+
+    for i in range(1, groups):
+        dispatch(lax.rem(me_e + i, groups)).start()
+    rows[me_t, me_e] = out_ref[me_e]
+
+    def forward(zt):
+        def one(i, _):
+            c = lax.rem(me_e + i, groups)
+
+            @pl.when(jnp.logical_or(zt != z, i > 0))
+            def _():
+                arrival(zt * COLUMNS + x, c).wait_recv()
+
+            @pl.when(jnp.logical_and(zt <= z, has_above))
+            def _():
+                gather(0, zt, c, above).start()
+
+            @pl.when(jnp.logical_and(zt >= z, has_below))
+            def _():
+                gather(1, zt, c, below).start()
+
+            gather(2, zt, c, partner).start()
+            return 0
+
+        lax.fori_loop(0, groups, one, 0)
+
+    def run_experts(t):
+        def one(l, _):
+            here = pl.ds(pl.multiple_of(l * capacity, capacity), capacity)
+            taken = rows[t, :, here, :].reshape(groups * capacity, width)
+            gate_val = jnp.dot(taken, wg[l], preferred_element_type=jnp.float32)
+            up_val = jnp.dot(taken, wu[l], preferred_element_type=jnp.float32)
+            active = (gate_val / (1.0 + jnp.exp(-gate_val)) * up_val).astype(jnp.bfloat16)
+            given = jnp.dot(active, wd[l], preferred_element_type=jnp.float32)
+            part[t, :, here, :] = given.astype(jnp.bfloat16).reshape(groups, capacity, width)
+            return 0
+
+        lax.fori_loop(0, experts, one, 0)
+
+    def stage(it, _):
+        @pl.when(it < depth)
+        def _():
+            forward(lookup(order, z, it))
+
+        @pl.when(it == 0)
+        def _():
+            for copy in weight_copies:
+                copy.wait()
+
+        def side(h, _):
+            at = it - h
+
+            @pl.when(jnp.logical_and(at >= 0, at < depth))
+            def _():
+                zt = lookup(order, z, at)
+                t = zt * COLUMNS + x + h * (1 - 2 * x)
+
+                @pl.when(h == 1)
+                def _():
+                    def one(i, _):
+                        arrival(t, lax.rem(me_e + i, groups)).wait_recv()
+                        return 0
+
+                    lax.fori_loop(0, groups, one, 0)
+
+                run_experts(t)
+
+            return 0
+
+        lax.fori_loop(0, 2, side, 0)
+        return 0
+
+    lax.fori_loop(0, depth + 1, stage, 0)
+
+    def start_x(k, _):
+        zt = lookup(order, z, depth - 1 - k)
+
+        def one(i, _):
+            x_sum(zt, lax.rem(me_e + i, groups)).start()
+            return 0
+
+        return lax.fori_loop(0, groups, one, 0)
+
+    lax.fori_loop(0, depth, start_x, 0)
+
+    def reduce_target(k, _):
+        zt = lookup(order, z, depth - 1 - k)
+        t = zt * COLUMNS + x
+
+        def one(i, _):
+            c = lax.rem(me_e + i, groups)
+            x_sum(zt, c).wait_recv()
+            total = part[t, c].astype(jnp.float32) + from_x[zt, c].astype(jnp.float32)
+            part[t, c] = total.astype(jnp.bfloat16)
+
+            @pl.when(jnp.logical_and(zt >= z, has_below))
+            def _():
+                z_sum(0, zt, c, partner).wait_recv()
+                part[t, c] = (
+                    part[t, c].astype(jnp.float32) + from_z[0, zt, c].astype(jnp.float32)
+                ).astype(jnp.bfloat16)
+
+            @pl.when(jnp.logical_and(zt <= z, has_above))
+            def _():
+                z_sum(1, zt, c, partner).wait_recv()
+                part[t, c] = (
+                    part[t, c].astype(jnp.float32) + from_z[1, zt, c].astype(jnp.float32)
+                ).astype(jnp.bfloat16)
+
+            @pl.when(zt > z)
+            def _():
+                z_sum(0, zt, c, above).start()
+
+            @pl.when(zt < z)
+            def _():
+                z_sum(1, zt, c, below).start()
+
+            @pl.when(jnp.logical_and(zt == z, i > 0))
+            def _():
+                send_back(c).start()
+
+            @pl.when(jnp.logical_and(zt == z, i == 0))
+            def _():
+                back_ref[c] = part[t, c]
+
+            return 0
+
+        return lax.fori_loop(0, groups, one, 0)
+
+    lax.fori_loop(0, depth, reduce_target, 0)
+
+    def finish(zt, _):
+        def one(c, _):
+            @pl.when(jnp.logical_and(zt <= z, has_above))
+            def _():
+                gather(0, zt, c, above).wait_send()
+
+            @pl.when(jnp.logical_and(zt >= z, has_below))
+            def _():
+                gather(1, zt, c, below).wait_send()
+
+            gather(2, zt, c, partner).wait_send()
+            x_sum(zt, c).wait_send()
+
+            @pl.when(zt != z)
+            def _():
+                z_sum(0, zt, c, partner).wait_send()
+
+            return 0
+
+        return lax.fori_loop(0, groups, one, 0)
+
+    lax.fori_loop(0, depth, finish, 0)
+    for i in range(1, groups):
+        c = lax.rem(me_e + i, groups)
+        dispatch(c).wait_send()
+        send_back(c).wait_send()
+        back_arrival(c).wait_recv()
+        back_ref[c] = back[c]
+
+
+def expert_exchange(outgoing, w_gate, w_up, w_down, capacity):
+    groups, slots, width = outgoing.shape
+    tp = lax.axis_size("tp")
+    depth = tp // COLUMNS
+    experts, _, hidden_units = w_gate.shape
+    dma = pltpu.SemaphoreType.DMA
+    chunk = (groups, slots, width)
+    kind = outgoing.dtype
+    rows_all = groups * capacity * tp * experts
+    return pl.pallas_call(
+        functools.partial(expert_kernel, groups, depth, capacity),
+        out_shape=jax.ShapeDtypeStruct(outgoing.shape, kind),
+        in_specs=[pl.BlockSpec(memory_space=pltpu.VMEM)]
+        + [pl.BlockSpec(memory_space=pl.ANY)] * 3,
+        out_specs=pl.BlockSpec(memory_space=pltpu.VMEM),
+        scratch_shapes=[
+            pltpu.VMEM(w_gate.shape, kind),
+            pltpu.VMEM(w_up.shape, kind),
+            pltpu.VMEM(w_down.shape, kind),
+            pltpu.VMEM((tp,) + chunk, kind),
+            pltpu.VMEM((tp,) + chunk, kind),
+            pltpu.VMEM((depth,) + chunk, kind),
+            pltpu.VMEM((2, depth) + chunk, kind),
+            pltpu.VMEM(chunk, kind),
+            dma((3,)),
+            dma((groups,)),
+            dma((3, depth, groups)),
+            dma((tp, groups)),
+            dma((depth, groups)),
+            dma((depth, groups)),
+            dma((depth, groups)),
+            dma((2, depth, groups)),
+            dma((groups,)),
+            dma((groups,)),
+        ],
+        compiler_params=pltpu.CompilerParams(
+            collective_id=0, has_side_effects=True, vmem_limit_bytes=VMEM_BYTES
+        ),
+        cost_estimate=pl.CostEstimate(
+            flops=6 * rows_all * width * hidden_units,
+            bytes_accessed=3 * w_gate.size * 2,
+            transcendentals=rows_all * hidden_units,
+        ),
+    )(outgoing, w_gate, w_up, w_down)
+
+
+def expert_collectives(outgoing, w_gate, w_up, w_down, capacity):
+    groups, slots, width = outgoing.shape
+    experts = w_gate.shape[0]
+    arrived = lax.all_to_all(outgoing, "ep", split_axis=0, concat_axis=0, tiled=True)
+    gathered = lax.all_gather(
+        arrived.reshape(groups, experts, capacity, width), "tp", axis=0, tiled=True
+    )
+    gate_val = jnp.einsum("recd,edf->recf", gathered, w_gate, preferred_element_type=jnp.float32)
+    up_val = jnp.einsum("recd,edf->recf", gathered, w_up, preferred_element_type=jnp.float32)
+    active = (jax.nn.silu(gate_val) * up_val).astype(jnp.bfloat16)
+    given = jnp.einsum("recf,efd->recd", active, w_down, preferred_element_type=jnp.float32)
+    summed = lax.psum_scatter(
+        given.astype(jnp.bfloat16), "tp", scatter_dimension=0, tiled=True
+    ).reshape(groups, slots, width)
+    return lax.all_to_all(summed, "ep", split_axis=0, concat_axis=0, tiled=True)
 
 
 def attend(query_part, key_part, value_part):
@@ -55,30 +382,22 @@
     slots = slot_index.reshape(tokens, 2)
     gates = route_gates.reshape(tokens, 2)
     valid = slots >= 0
-    slot_target = jnp.where(valid, slots, capacity)
-    spread_rows = jnp.broadcast_to(normed[:, None, :], (tokens, 2, model_width))
+    row_target = jnp.where(valid, chosen * capacity + slots, -1)
+    row_ids = jnp.arange(experts_all * capacity, dtype=jnp.int32)
+    picks = row_target[:, :, None] == row_ids
+    spread = jnp.any(picks, axis=1).astype(jnp.bfloat16)
     outgoing = (
-        jnp.zeros((capacity, experts_all, model_width), jnp.bfloat16)
-        .at[slot_target, chosen]
-        .set(spread_rows, mode="drop")
-    )
-    arrived = lax.all_to_all(outgoing, "ep", split_axis=1, concat_axis=0, tiled=True)
-    gathered = lax.all_gather(arrived, "tp", axis=0, tiled=True)
-    gate_val = jnp.einsum("red,edf->ref", gathered, w_gate, preferred_element_type=jnp.float32)
-    up_val = jnp.einsum("red,edf->ref", gathered, w_up, preferred_element_type=jnp.float32)
-    active = (jax.nn.silu(gate_val) * up_val).astype(jnp.bfloat16)
-    summed = lax.psum_scatter(
-        jnp.einsum("ref,efd->red", active, w_down, preferred_element_type=jnp.float32).astype(
-            jnp.bfloat16
-        ),
-        "tp",
-        scatter_dimension=0,
-        tiled=True,
-    )
-    returned = lax.all_to_all(summed, "ep", split_axis=0, concat_axis=1, tiled=True)
-    picked = returned[jnp.where(valid, slots, 0), chosen]
+        jnp.einsum("tr,td->rd", spread, normed, preferred_element_type=jnp.float32)
+        .astype(jnp.bfloat16)
+        .reshape(groups, experts_local * capacity, model_width)
+    )
+    exchange = expert_exchange if lax.axis_size("tp") == 4 * COLUMNS else expert_collectives
+    returned = exchange(outgoing, w_gate, w_up, w_down, capacity).reshape(-1, model_width)
+    picked = jnp.einsum(
+        "tcr,rd->ctd", picks.astype(jnp.bfloat16), returned, preferred_element_type=jnp.float32
+    )
     weights = jnp.where(valid, gates, 0.0)
-    combined = hidden + jnp.sum(weights[:, :, None] * picked.astype(jnp.float32), axis=1)
+    combined = hidden + (weights[:, :1] * picked[0] + weights[:, 1:] * picked[1])
     return combined.reshape(frames_local, sites_local, model_width).astype(jnp.bfloat16)
 
 

time: 410 us -> 223 us (0.54)
  waiting for transfers between devices: 260 us -> 21.8 us
  Pallas kernels: 0 us -> 170 us
  blocking collectives: 34.7 us -> 0 us
  matrix products: 41.9 us -> 8.27 us
  local copies, waits for them, and re-layouts: 42.3 us -> 9.04 us
  between operations: 13.6 us -> 0.14 us
    pallas_call x0 -> x1, Pallas kernels: none -> 170 us  [expert_exchange(): pl.pallas_call(functools.partial(expert_kernel, groups, depth, capacity),...]
    reduce_scatter x1 -> x0, waiting for transfers between devices: 132 us -> none  [body(): lax.psum_scatter(jnp.einsum('ref,efd->red', active, w_down, preferred_ele...]
    all_gather x1 -> x0, waiting for transfers between devices: 111 us -> none  [body(): gathered = lax.all_gather(arrived, 'tp', axis=0, tiled=True)]
    all_to_all x2 -> x0, blocking collectives: 34.7 us -> none  [the longest x1 19.2 us: body(): lax.all_to_all(split_view, 'ep', split_axis=1, concat_axis=0, tiled=True)]
    dot_general x2, matrix products: 36.4 us -> 3.01 us  [the longest x1 1.63 us: body(): jnp.einsum('tcr,rd->ctd', picks.astype(jnp.bfloat16), returned, preferred...]
    scatter x2 -> x0, local copies, waits for them, and re-layouts: 21.1 us -> none  [body(): outgoing = jnp.zeros((capacity, experts_all, model_width), jnp.bfloat16)....]
    all_to_all x1, waiting for transfers between devices: 10.6 us -> 16 us  [body(): lax.all_to_all(split_view, 'ep', split_axis=1, concat_axis=0, tiled=True)]
    gather x1 -> x0, local copies, waits for them, and re-layouts: 4.73 us -> none  [body(): picked = returned[jnp.where(valid, slots, 0), chosen]]
  transfers between devices with their start and end apart: 4 -> 2, of which waited for: 4 -> 2; matrix products, arithmetic and copies ran while one was open for 0% -> 0% of each run, Pallas kernels for 0% -> 0%
where the time goes in v1:
time: 223 us; the launch traced here: 221 us
  Pallas kernels  170 us (76%)
  waiting for transfers between devices  21.8 us (10%)
  starting transfers between devices  9.81 us (4%)
  local copies, waits for them, and re-layouts  9.04 us (4%)
  matrix products  8.27 us (4%)
    pallas_call x1, Pallas kernels, expert_exchange(): pl.pallas_call(functools.partial(expert_kernel, groups, depth, capacity),...  170 us
    all_to_all x1, waiting for transfers between devices, body(): lax.all_to_all(split_view, 'ep', split_axis=1, concat_axis=0, tiled=True)  16 us
    all_to_all x1, waiting for transfers between devices, body(): lax.all_to_all(by_sites, 'ep', split_axis=0, concat_axis=1, tiled=True)  5.83 us
    all_to_all x1, starting transfers between devices, body(): lax.all_to_all(by_sites, 'ep', split_axis=0, concat_axis=1, tiled=True)  5.35 us
    all_to_all x1, starting transfers between devices, body(): lax.all_to_all(split_view, 'ep', split_axis=1, concat_axis=0, tiled=True)  4.47 us
  transfers between devices with their start and end apart: 2, of which 2 were waited for; matrix products, arithmetic and copies ran while one was open for 0% of the time, Pallas kernels for 0%

profile of v1, /device:TPU:13, one launch (start us, length us, event | category | flops | bytes accessed | tf_op | source)
XLA Modules:
  0.0 220.7 jit_solution(14073496062524291667)
XLA Ops:
  0.0 2.5 %copy.27 = bf16[4,4,8,3,1792]{4,2,3,0,1:T(8,128)(2,1)} copy(bf16[4,4,8,3,1792]{4,2,1,3,0:T(8,128)(2,1)} %bitcast.56) | data formatting | bytes 2752512 | tf_op jit(solution)/shard_map/reshape | solution.py:362
  2.5 0.0 copy-start.2
  2.5 0.0 copy-start.4
  2.5 4.5 %all-to-all-start = ((bf16[4,4,8,3,1792]{4,2,3,0,1:T(8,128)(2,1)}), bf16[4,4,8,3,1792]{4,2,3,0,1:T(8,128)(2,1)S(1)}, u32[]{:S(2)}, u32[]{:S(2)}) async-start(bf16[4,4,8,3,1792]{4,2,3,0,1:T(8,128)(2,1)} %copy.27), calls=%async_computation | async-start | bytes 2752512 | tf_op jit(solution)/shard_map/all_to_all | solution.py:365
  7.0 0.0 copy-done.2
  7.0 0.0 copy-done.4
  7.0 0.1 select_n.21
  7.1 16.0 %all-to-all-done = bf16[4,4,8,3,1792]{4,2,3,0,1:T(8,128)(2,1)S(1)} async-done(((bf16[4,4,8,3,1792]{4,2,3,0,1:T(8,128)(2,1)}), bf16[4,4,8,3,1792]{4,2,3,0,1:T(8,128)(2,1)S(1)}, u32[]{:S(2)}, u32[]{:S(2)}) %all-to-all-start) | async-done | bytes 1376288 | tf_op jit(solution)/shard_map/all_to_all | solution.py:365
  23.1 0.1 fusion.27
  23.1 1.0 reshape_squeeze.10
  24.2 1.0 reshape_squeeze.9
  25.2 2.0 reshape_squeeze.11
  27.2 0.0 copy-start
  27.2 2.9 %fusion.28 = (f32[8,28,16]{2,1,0:T(8,128)S(1)}, f32[8,28,16,16]{2,3,1,0:T(8,128)}) fusion(bf16[16,8,28,64]{3,2,1,0:T(8,128)(2,1)S(1)} %reshape_squeeze.10, bf16[16,8,28,64]{3,2,1,0:T(8,128)(2,1)S(1)} %reshape_squeeze.9), kind=kOutput, calls=%fused_computation.34 | convolution fusion | flops 7512079 | bytes 1161216 | tf_op jit(solution)/shard_map/sub | solution.py:348
  30.1 0.0 copy-done
  30.1 2.3 %fusion.2 = bf16[16,8,28,64]{3,0,2,1:T(8,128)(2,1)S(1)} fusion(f32[8,28,16,16]{2,3,1,0:T(8,128)} %get-tuple-element.15, bf16[16,8,28,64]{3,2,1,0:T(8,128)(2,1)S(1)} %copy-done, f32[8,28,16]{2,1,0:T(8,128)S(1)} %get-tuple-element.14), kind=kOutput, calls=%fused_computation.8 | convolution fusion | flops 7684096 | bytes 1161216 | tf_op jit(solution)/shard_map/shfg,gshd->fshd/dot_general | solution.py:351
  32.4 0.0 copy-start.5
  32.4 0.0 copy-start.1
  32.5 0.3 copy.32
  32.7 0.0 copy-start.3
  32.7 1.6 convert_element_type.49
  34.3 5.3 %all-to-all-start.1 = ((bf16[16,1,8,1792]{3,2,1,0:T(8,128)(2,1)}), bf16[16,1,8,1792]{3,2,1,0:T(8,128)(2,1)S(1)}, u32[]{:S(2)}, u32[]{:S(2)}) async-start(bf16[16,1,8,1792]{3,2,1,0:T(8,128)(2,1)} %bitcast.7), calls=%async_computation.1 | async-start | bytes 917504 | tf_op jit(solution)/shard_map/all_to_all | solution.py:369
  39.7 0.0 copy-done.5
  39.7 0.1 select_n.19
  39.8 0.1 mul.53
  39.9 0.1 mul.63
  40.0 0.1 fusion.11
  40.1 5.8 %all-to-all-done.1 = bf16[16,1,8,1792]{3,2,1,0:T(8,128)(2,1)S(1)} async-done(((bf16[16,1,8,1792]{3,2,1,0:T(8,128)(2,1)}), bf16[16,1,8,1792]{3,2,1,0:T(8,128)(2,1)S(1)}, u32[]{:S(2)}, u32[]{:S(2)}) %all-to-all-start.1) | async-done | bytes 458784 | tf_op jit(solution)/shard_map/all_to_all | solution.py:369
  45.9 0.0 copy-done.1
  45.9 0.2 multiply_reduce_fusion.1
  46.2 0.1 rsqrt.12
  46.2 0.0 copy-done.3
  46.3 0.2 fusion.4
  46.4 1.4 convolution_convert_fusion
  47.8 170.1 %shard_map.91 = bf16[4,64,1792]{2,1,0:T(8,128)(2,1)} custom-call(bf16[4,64,1792]{2,1,0:T(8,128)(2,1)} %bitcast.57, bf16[2,1792,896]{2,1,0:T(8,128)(2,1)} %wg_hbm.1, bf16[2,1792,896]{2,1,0:T(8,128)(2,1)} %wu_hbm.1, bf16[2,896,1792]{2,1,0:T(8,128)(2,1)} %wd_hbm.1), custom_call_target="tpu_custom_call" | custom-call | flops 19730006016 | bytes 19267584 | tf_op jit(solution)/shard_map/pallas_call | solution.py:284
  217.9 1.6 convolution_bitcast_fusion
  219.6 0.1 fusion.26
  219.7 1.0 add_convert_fusion
  (6 shorter events, 0.0 us)
Async XLA Ops:
  2.5 4.5 %copy-start.2 = (s32[4,32,2]{1,2,0:T(2,128)S(1)}, s32[4,32,2]{1,2,0:T(2,128)}, u32[]{:S(2)}) copy-start(s32[4,32,2]{1,2,0:T(2,128)} %param.14) | copy-start | bytes 3076
  2.5 4.5 %copy-start.4 = (s32[4,32,2]{1,2,0:T(2,128)S(1)}, s32[4,32,2]{1,2,0:T(2,128)}, u32[]{:S(2)}) copy-start(s32[4,32,2]{1,2,0:T(2,128)} %param.12) | copy-start | bytes 3076
  2.5 20.5 %all-to-all-start = ((bf16[4,4,8,3,1792]{4,2,3,0,1:T(8,128)(2,1)}), bf16[4,4,8,3,1792]{4,2,3,0,1:T(8,128)(2,1)S(1)}, u32[]{:S(2)}, u32[]{:S(2)}) async-start(bf16[4,4,8,3,1792]{4,2,3,0,1:T(8,128)(2,1)} %copy.27), calls=%async_computation | async-start | bytes 2752512 | tf_op jit(solution)/shard_map/all_to_all | solution.py:365
  27.2 2.9 %copy-start = (bf16[16,8,28,64]{3,2,1,0:T(8,128)(2,1)S(1)}, bf16[16,8,28,64]{3,2,1,0:T(8,128)(2,1)}, u32[]{:S(2)}) copy-start(bf16[16,8,28,64]{3,2,1,0:T(8,128)(2,1)} %reshape_squeeze.11) | copy-start | bytes 1376260
  32.4 7.2 %copy-start.5 = (f32[4,32,2]{1,2,0:T(2,128)S(1)}, f32[4,32,2]{1,2,0:T(2,128)}, u32[]{:S(2)}) copy-start(f32[4,32,2]{1,2,0:T(2,128)} %param.13) | copy-start | bytes 3076
  32.4 13.5 %copy-start.1 = (bf16[4,32,1792]{2,1,0:T(8,128)(2,1)S(1)}, bf16[4,32,1792]{2,1,0:T(8,128)(2,1)}, u32[]{:S(2)}) copy-start(bf16[4,32,1792]{2,1,0:T(8,128)(2,1)} %param.10) | copy-start | bytes 1376260
  32.7 13.5 %copy-start.3 = (f32[1792]{0:T(1024)S(1)}, f32[1792]{0:T(1024)}, u32[]{:S(2)}) copy-start(f32[1792]{0:T(1024)} %param.11) | copy-start | bytes 21508
  34.3 11.6 %all-to-all-start.1 = ((bf16[16,1,8,1792]{3,2,1,0:T(8,128)(2,1)}), bf16[16,1,8,1792]{3,2,1,0:T(8,128)(2,1)S(1)}, u32[]{:S(2)}, u32[]{:S(2)}) async-start(bf16[16,1,8,1792]{3,2,1,0:T(8,128)(2,1)} %bitcast.7), calls=%async_computation.1 | async-start | bytes 917504 | tf_op jit(solution)/shard_map/all_to_all | solution.py:369

commit v2 on v1

--- a/solution.py
+++ b/solution.py
@@ -44,6 +44,7 @@
     experts = wg.shape[0]
     width = rows.shape[-1]
     order = near_first(depth)
+    sums = [[row[-2], row[-1]] + row[-3::-1] for row in order]
 
     weight_copies = [
         pltpu.make_async_copy(src, dst, w_sem.at[i])
@@ -150,6 +151,15 @@
 
         lax.fori_loop(0, experts, one, 0)
 
+    def start_x(k, _):
+        zt = lookup(sums, z, k)
+
+        def one(i, _):
+            x_sum(zt, lax.rem(me_e + i, groups)).start()
+            return 0
+
+        return lax.fori_loop(0, groups, one, 0)
+
     def stage(it, _):
         @pl.when(it < depth)
         def _():
@@ -159,6 +169,10 @@
         def _():
             for copy in weight_copies:
                 copy.wait()
+
+        @pl.when(it == depth)
+        def _():
+            start_x(0, 0)
 
         def side(h, _):
             at = it - h
@@ -185,19 +199,10 @@
 
     lax.fori_loop(0, depth + 1, stage, 0)
 
-    def start_x(k, _):
-        zt = lookup(order, z, depth - 1 - k)
-
-        def one(i, _):
-            x_sum(zt, lax.rem(me_e + i, groups)).start()
-            return 0
-
-        return lax.fori_loop(0, groups, one, 0)
-
-    lax.fori_loop(0, depth, start_x, 0)
+    lax.fori_loop(1, depth, start_x, 0)
 
     def reduce_target(k, _):
-        zt = lookup(order, z, depth - 1 - k)
+        zt = lookup(sums, z, k)
         t = zt * COLUMNS + x
 
         def one(i, _):
@@ -335,21 +340,140 @@
     return lax.all_to_all(summed, "ep", split_axis=0, concat_axis=0, tiled=True)
 
 
-def attend(query_part, key_part, value_part):
-    frames_q, site_count, model_width = query_part.shape
-    frames_k = key_part.shape[0]
-    head_count = model_width // HD
-    query_h = query_part.reshape(frames_q, site_count, head_count, HD)
-    key_h = key_part.reshape(frames_k, site_count, head_count, HD)
-    value_h = value_part.reshape(frames_k, site_count, head_count, HD)
-    scores = jnp.einsum(
-        "fshd,gshd->shfg", query_h, key_h, preferred_element_type=jnp.float32
-    ) / math.sqrt(HD)
-    scores = scores - jnp.max(scores, axis=-1, keepdims=True)
-    expo = jnp.exp(scores)
-    probs = (expo / jnp.sum(expo, axis=-1, keepdims=True)).astype(jnp.bfloat16)
-    mixed = jnp.einsum("shfg,gshd->fshd", probs, value_h, preferred_element_type=jnp.float32)
-    return mixed.reshape(frames_q, site_count, model_width).astype(jnp.bfloat16)
+def attention_kernel(groups, sites, qkv_ref, out_ref, qkv, mixed, back, send, recv, back_send, back_recv):
+    me_e = lax.axis_index("ep")
+    me_t = lax.axis_index("tp")
+    rows = out_ref.shape[1]
+    width = out_ref.shape[2]
+    tokens = groups * rows
+    pieces = send.shape[1]
+    span = width // pieces
+
+    barrier = pltpu.get_barrier_semaphore()
+    for i in range(1, groups):
+        pl.semaphore_signal(
+            barrier, inc=1, device_id=(lax.rem(me_e + i, groups), me_t), device_id_type=MESH
+        )
+    pl.semaphore_wait(barrier, groups - 1)
+
+    def columns(p):
+        return pl.ds(pl.multiple_of(p * span, span), span)
+
+    def remote(src, dst, send_sem, recv_sem, to_e):
+        return pltpu.make_async_remote_copy(
+            src_ref=src, dst_ref=dst, send_sem=send_sem, recv_sem=recv_sem,
+            device_id=(to_e, me_t), device_id_type=MESH,
+        )
+
+    def give(e, p):
+        here = columns(p)
+        return remote(
+            qkv_ref.at[e, :, here], qkv.at[me_e, :, here], send.at[e, p], recv.at[me_e, p], e
+        )
+
+    def take(e, p):
+        here = columns(p)
+        return remote(qkv_ref.at[e, :, here], qkv.at[e, :, here], send.at[e, p], recv.at[e, p], e)
+
+    def give_back(e, p):
+        here = columns(p)
+        return remote(
+            mixed.at[e, :, here], back.at[me_e, :, here], back_send.at[e, p],
+            back_recv.at[me_e, p], e,
+        )
+
+    def take_back(e, p):
+        here = columns(p)
+        return remote(
+            mixed.at[e, :, here], back.at[e, :, here], back_send.at[e, p], back_recv.at[e, p], e
+        )
+
+    def start(p, _):
+        for i in range(1, groups):
+            give(lax.rem(me_e + i, groups), p).start()
+        return 0
+
+    lax.fori_loop(0, pieces, start, 0)
+    qkv[me_e] = qkv_ref[me_e]
+
+    row_site = lax.broadcasted_iota(jnp.int32, (tokens, tokens), 0) % sites
+    column_site = lax.broadcasted_iota(jnp.int32, (tokens, tokens), 1) % sites
+    same = row_site == column_site
+    pair = 2 * HD
+    lane = lax.broadcasted_iota(jnp.int32, (tokens, pair), 1)
+    first = lane < HD
+    keep = (first.astype(jnp.bfloat16), jnp.logical_not(first).astype(jnp.bfloat16))
+
+    def attend(p, _):
+        for i in range(1, groups):
+            take(lax.rem(me_e + i, groups), p).wait_recv()
+        for j in range(span // pair):
+            here = pl.ds(pl.multiple_of(p * span + j * pair, pair), pair)
+            query, key, value = (
+                qkv[:, n * rows : (n + 1) * rows, here].reshape(tokens, pair) for n in range(3)
+            )
+            halves = []
+            for mask in keep:
+                scores = lax.dot_general(
+                    query * mask, key, (((1,), (1,)), ((), ())),
+                    preferred_element_type=jnp.float32,
+                ) / math.sqrt(HD)
+                scores = jnp.where(same, scores, -jnp.inf)
+                expo = jnp.exp(scores - jnp.max(scores, axis=-1, keepdims=True))
+                probs = (expo / jnp.sum(expo, axis=-1, keepdims=True)).astype(jnp.bfloat16)
+                halves.append(jnp.dot(probs, value, preferred_element_type=jnp.float32))
+            result = jnp.where(first, halves[0], halves[1]).astype(mixed.dtype)
+            mixed[:, :, here] = result.reshape(groups, rows, pair)
+        for i in range(1, groups):
+            give_back(lax.rem(me_e + i, groups), p).start()
+        return 0
+
+    lax.fori_loop(0, pieces, attend, 0)
+    out_ref[me_e] = mixed[me_e]
+
+    def finish(p, _):
+        for i in range(1, groups):
+            e = lax.rem(me_e + i, groups)
+            give(e, p).wait_send()
+            give_back(e, p).wait_send()
+            take_back(e, p).wait_recv()
+        return 0
+
+    lax.fori_loop(0, pieces, finish, 0)
+    for i in range(1, groups):
+        e = lax.rem(me_e + i, groups)
+        out_ref[e] = back[e]
+
+
+def attention_exchange(split_qkv, sites):
+    groups, rows_three, width = split_qkv.shape
+    pieces = width // (4 * HD)
+    dma = pltpu.SemaphoreType.DMA
+    shape = (groups, rows_three // 3, width)
+    tokens = groups * rows_three // 3
+    return pl.pallas_call(
+        functools.partial(attention_kernel, groups, sites),
+        out_shape=jax.ShapeDtypeStruct(shape, split_qkv.dtype),
+        in_specs=[pl.BlockSpec(memory_space=pltpu.VMEM)],
+        out_specs=pl.BlockSpec(memory_space=pltpu.VMEM),
+        scratch_shapes=[
+            pltpu.VMEM(split_qkv.shape, split_qkv.dtype),
+            pltpu.VMEM(shape, split_qkv.dtype),
+            pltpu.VMEM(shape, split_qkv.dtype),
+            dma((groups, pieces)),
+            dma((groups, pieces)),
+            dma((groups, pieces)),
+            dma((groups, pieces)),
+        ],
+        compiler_params=pltpu.CompilerParams(
+            collective_id=1, has_side_effects=True, vmem_limit_bytes=VMEM_BYTES // 2
+        ),
+        cost_estimate=pl.CostEstimate(
+            flops=8 * tokens * tokens * width,
+            bytes_accessed=split_qkv.size * 3,
+            transcendentals=tokens * tokens * width // HD,
+        ),
+    )(split_qkv)
 
 
 def body(
@@ -359,15 +483,17 @@
     sites_local = residual.shape[1]
     model_width = residual.shape[2]
     groups = lax.axis_size("ep")
-    split_view = query_key_value.reshape(
-        frames_local, groups, sites_local // groups, 3, model_width
-    )
-    site_block = lax.all_to_all(split_view, "ep", split_axis=1, concat_axis=0, tiled=True)
-    by_sites = attend(site_block[:, 0, :, 0], site_block[:, 0, :, 1], site_block[:, 0, :, 2])[
-        :, None
-    ]
-    attended = lax.all_to_all(by_sites, "ep", split_axis=0, concat_axis=1, tiled=True).reshape(
-        frames_local, sites_local, model_width
+    sites = sites_local // groups
+    split_qkv = (
+        query_key_value.reshape(frames_local, groups, sites, 3, model_width)
+        .transpose(1, 3, 0, 2, 4)
+        .reshape(groups, 3 * frames_local * sites, model_width)
+    )
+    attended = (
+        attention_exchange(split_qkv, sites)
+        .reshape(groups, frames_local, sites, model_width)
+        .transpose(1, 0, 2, 3)
+        .reshape(frames_local, sites_local, model_width)
     )
     tokens = frames_local * sites_local
     hidden = (residual.astype(jnp.float32) + attended.astype(jnp.float32)).reshape(

time: 223 us -> 207 us (0.928); the launches traced: 221 us -> 207 us
  Pallas kernels: 170 us -> 200 us
  waiting for transfers between devices: 21.8 us -> 0 us
  starting transfers between devices: 9.81 us -> 0 us
  local copies, waits for them, and re-layouts: 9.04 us -> 2.86 us
  matrix products: 8.27 us -> 3.01 us
    pallas_call x0 -> x1, Pallas kernels: none -> 23.9 us  [attention_exchange(): pl.pallas_call(functools.partial(attention_kernel, groups, sites), out_sh...]
    all_to_all x2 -> x0, waiting for transfers between devices: 21.8 us -> none  [the longest x1 16 us: body(): lax.all_to_all(split_view, 'ep', split_axis=1, concat_axis=0, tiled=True)]
    all_to_all x2 -> x0, starting transfers between devices: 9.81 us -> none  [the longest x1 5.35 us: body(): lax.all_to_all(by_sites, 'ep', split_axis=0, concat_axis=1, tiled=True)]
    pallas_call x1, Pallas kernels: 170 us -> 176 us  [expert_exchange(): pl.pallas_call(functools.partial(expert_kernel, groups, depth, capacity),...]
    another operation x3 -> x0, local copies, waits for them, and re-layouts: 4 us -> none  [the longest x1 1.99 us: attend(): value_h = value_part.reshape(frames_k, site_count, head_count, HD)]
    sub x1 -> x0, matrix products: 2.94 us -> none  [attend(): scores = scores - jnp.max(scores, axis=-1, keepdims=True)]
    dot_general x1 -> x0, matrix products: 2.32 us -> none  [attend(): jnp.einsum('shfg,gshd->fshd', probs, value_h, preferred_element_type=jnp....]
  transfers between devices with their start and end apart: 2 -> 0, of which waited for: 2 -> 0; matrix products, arithmetic and copies ran while one was open for 0% -> 0% of each run, Pallas kernels for 0% -> 0%
where the time goes in v2:
time: 207 us
  Pallas kernels  200 us (97%)
  matrix products  3.01 us (1%)
  local copies, waits for them, and re-layouts  2.86 us (1%)
    pallas_call x1, Pallas kernels, expert_exchange(): pl.pallas_call(functools.partial(expert_kernel, groups, depth, capacity),...  176 us
    pallas_call x1, Pallas kernels, attention_exchange(): pl.pallas_call(functools.partial(attention_kernel, groups, sites), out_sh...  23.9 us

profile of v2, /device:TPU:13, one launch (start us, length us, event | category | flops | bytes accessed | tf_op | source)
XLA Modules:
  0.0 207.1 jit_solution(13570401427598094494)
XLA Ops:
  0.0 0.0 copy-start
  0.0 1.5 copy.12
  1.5 0.0 copy-start.2
  1.5 23.9 %shard_map.91 = bf16[4,32,1792]{2,1,0:T(8,128)(2,1)S(1)} custom-call(bf16[4,96,1792]{2,1,0:T(8,128)(2,1)S(1)} %bitcast.35), custom_call_target="tpu_custom_call" | custom-call | flops 234881024 | bytes 2064384 | tf_op jit(solution)/shard_map/pallas_call | solution.py:454
  25.4 0.0 copy-done
  25.4 0.0 copy-start.1
  25.4 0.0 copy-start.3
  25.5 0.2 multiply_reduce_fusion
  25.7 0.1 rsqrt.12
  25.8 0.0 copy-done.2
  25.8 0.1 fusion.1
  25.9 0.2 copy-done.1
  26.1 0.0 copy-done.3
  26.2 0.1 select_n.21
  26.2 0.1 fusion.2
  26.4 1.4 convolution_convert_fusion
  27.7 175.8 %shard_map.92 = bf16[4,64,1792]{2,1,0:T(8,128)(2,1)} custom-call(bf16[4,64,1792]{2,1,0:T(8,128)(2,1)} %bitcast.39, bf16[2,1792,896]{2,1,0:T(8,128)(2,1)} %wg_hbm.1, bf16[2,1792,896]{2,1,0:T(8,128)(2,1)} %wu_hbm.1, bf16[2,896,1792]{2,1,0:T(8,128)(2,1)} %wd_hbm.1), custom_call_target="tpu_custom_call" | custom-call | flops 19730006016 | bytes 19267584 | tf_op jit(solution)/shard_map/pallas_call | solution.py:289
  203.5 1.6 convolution_bitcast_fusion
  205.2 0.0 copy-start.4
  205.2 0.1 fusion.4
  205.3 0.5 copy-done.4
  205.9 0.1 select_n.19
  206.0 0.1 mul.53
  206.1 0.1 mul.63
  206.1 1.0 add_convert_fusion
  (6 shorter events, 0.1 us)
Async XLA Ops:
  0.0 25.4 %copy-start = (bf16[4,32,1792]{2,1,0:T(8,128)(2,1)S(1)}, bf16[4,32,1792]{2,1,0:T(8,128)(2,1)}, u32[]{:S(2)}) copy-start(bf16[4,32,1792]{2,1,0:T(8,128)(2,1)} %param.10) | copy-start | bytes 1376260
  1.5 24.3 %copy-start.2 = (f32[1792]{0:T(1024)S(1)}, f32[1792]{0:T(1024)}, u32[]{:S(2)}) copy-start(f32[1792]{0:T(1024)} %param.11) | copy-start | bytes 21508
  25.4 0.7 copy-start.1
  25.4 0.7 copy-start.3
  205.2 0.7 copy-start.4

commit v3 on v2

--- a/solution.py
+++ b/solution.py
@@ -29,8 +29,9 @@
 
 def expert_kernel(
     groups, depth, capacity, out_ref, wg_hbm, wu_hbm, wd_hbm, back_ref,
-    wg, wu, wd, rows, part, from_x, from_z, back,
-    w_sem, disp_send, ag_send, ag_recv, x_send, x_recv, z_send, z_recv, back_send, back_recv,
+    wg, wu, wd, rows, part, from_x, from_z, from_z_cross, back,
+    w_sem, disp_send, ag_send, ag_recv, x_send, x_recv, z_send, z_recv,
+    cross_send, cross_recv, back_send, back_recv,
 ):
     me_e = lax.axis_index("ep")
     me_t = lax.axis_index("tp")
@@ -83,11 +84,9 @@
             (to_e, me_t),
         )
 
-    def gather(way, zt, c, to_t):
-        block = rows.at[zt * COLUMNS + x, c]
-        return remote(
-            block, block, ag_send.at[way, zt, c], ag_recv.at[zt * COLUMNS + x, c], (me_e, to_t)
-        )
+    def gather(way, t, c, to_t):
+        block = rows.at[t, c]
+        return remote(block, block, ag_send.at[way, t, c], ag_recv.at[t, c], (me_e, to_t))
 
     def arrival(t, c):
         block = rows.at[t, c]
@@ -105,6 +104,12 @@
             z_recv.at[way, zt, c], (me_e, to_t),
         )
 
+    def cross_sum(way, zt, to_t):
+        return remote(
+            part.at[zt * COLUMNS + (1 - x), me_e], from_z_cross.at[way, zt], cross_send.at[zt],
+            cross_recv.at[way, zt], (me_e, to_t),
+        )
+
     def send_back(c):
         return remote(
             part.at[me_t, c], back.at[me_e], back_send.at[c], back_recv.at[me_e], (c, me_t)
@@ -117,26 +122,37 @@
         dispatch(lax.rem(me_e + i, groups)).start()
     rows[me_t, me_e] = out_ref[me_e]
 
+    def along_z(zt, t, c):
+        @pl.when(jnp.logical_and(zt <= z, has_above))
+        def _():
+            gather(0, t, c, above).start()
+
+        @pl.when(jnp.logical_and(zt >= z, has_below))
+        def _():
+            gather(1, t, c, below).start()
+
     def forward(zt):
+        t = zt * COLUMNS + x
+
         def one(i, _):
             c = lax.rem(me_e + i, groups)
 
             @pl.when(jnp.logical_or(zt != z, i > 0))
             def _():
-                arrival(zt * COLUMNS + x, c).wait_recv()
-
-            @pl.when(jnp.logical_and(zt <= z, has_above))
-            def _():
-                gather(0, zt, c, above).start()
-
-            @pl.when(jnp.logical_and(zt >= z, has_below))
-            def _():
-                gather(1, zt, c, below).start()
-
-            gather(2, zt, c, partner).start()
+                arrival(t, c).wait_recv()
+
+            along_z(zt, t, c)
+
+            @pl.when(jnp.logical_or(zt == z, i > 0))
+            def _():
+                gather(2, t, c, partner).start()
+
             return 0
 
         lax.fori_loop(0, groups, one, 0)
+        across = zt * COLUMNS + (1 - x)
+        arrival(across, me_e).wait_recv()
+        along_z(zt, across, me_e)
 
     def run_experts(t):
         def one(l, _):
@@ -158,7 +174,7 @@
             x_sum(zt, lax.rem(me_e + i, groups)).start()
             return 0
 
-        return lax.fori_loop(0, groups, one, 0)
+        return lax.fori_loop(1, groups, one, 0)
 
     def stage(it, _):
         @pl.when(it < depth)
@@ -188,7 +204,7 @@
                         arrival(t, lax.rem(me_e + i, groups)).wait_recv()
                         return 0
 
-                    lax.fori_loop(0, groups, one, 0)
+                    lax.fori_loop(1, groups, one, 0)
 
                 run_experts(t)
 
@@ -200,30 +216,57 @@
     lax.fori_loop(0, depth + 1, stage, 0)
 
     lax.fori_loop(1, depth, start_x, 0)
+
+    def add(t, c, term):
+        total = part[t, c].astype(jnp.float32) + term.astype(jnp.float32)
+        part[t, c] = total.astype(jnp.bfloat16)
 
     def reduce_target(k, _):
         zt = lookup(sums, z, k)
         t = zt * COLUMNS + x
+        from_below = jnp.logical_and(zt >= z, has_below)
+        from_above = jnp.logical_and(zt <= z, has_above)
+        across = zt * COLUMNS + (1 - x)
+
+        @pl.when(from_below)
+        def _():
+            cross_sum(0, zt, partner).wait_recv()
+            add(across, me_e, from_z_cross[0, zt])
+
+        @pl.when(from_above)
+        def _():
+            cross_sum(1, zt, partner).wait_recv()
+            add(across, me_e, from_z_cross[1, zt])
+
+        @pl.when(zt > z)
+        def _():
+            cross_sum(0, zt, above).start()
+
+        @pl.when(zt < z)
+        def _():
+            cross_sum(1, zt, below).start()
+
+        @pl.when(zt == z)
+        def _():
+            x_sum(zt, me_e).start()
 
         def one(i, _):
             c = lax.rem(me_e + i, groups)
-            x_sum(zt, c).wait_recv()
-            total = part[t, c].astype(jnp.float32) + from_x[zt, c].astype(jnp.float32)
-            part[t, c] = total.astype(jnp.bfloat16)
-
-            @pl.when(jnp.logical_and(zt >= z, has_below))
+
+            @pl.when(jnp.logical_or(zt == z, i < groups))
+            def _():
+                x_sum(zt, c).wait_recv()
+                add(t, c, from_x[zt, c])
+
+            @pl.when(from_below)
             def _():
                 z_sum(0, zt, c, partner).wait_recv()
-                part[t, c] = (
-                    part[t, c].astype(jnp.float32) + from_z[0, zt, c].astype(jnp.float32)
-                ).astype(jnp.bfloat16)
-
-            @pl.when(jnp.logical_and(zt <= z, has_above))
+                add(t, c, from_z[0, zt, c])
+
+            @pl.when(from_above)
             def _():
                 z_sum(1, zt, c, partner).wait_recv()
-                part[t, c] = (
-                    part[t, c].astype(jnp.float32) + from_z[1, zt, c].astype(jnp.float32)
-                ).astype(jnp.bfloat16)
+                add(t, c, from_z[1, zt, c])
 
             @pl.when(zt > z)
             def _():
@@ -233,32 +276,45 @@
             def _():
                 z_sum(1, zt, c, below).start()
 
-            @pl.when(jnp.logical_and(zt == z, i > 0))
+            @pl.when(jnp.logical_and(zt == z, i < groups))
             def _():
                 send_back(c).start()
 
-            @pl.when(jnp.logical_and(zt == z, i == 0))
+            @pl.when(jnp.logical_and(zt == z, i == groups))
             def _():
                 back_ref[c] = part[t, c]
 
             return 0
 
-        return lax.fori_loop(0, groups, one, 0)
+        return lax.fori_loop(1, groups + 1, one, 0)
 
     lax.fori_loop(0, depth, reduce_target, 0)
 
+    def sent(zt, t, c):
+        @pl.when(jnp.logical_and(zt <= z, has_above))
+        def _():
+            gather(0, t, c, above).wait_send()
+
+        @pl.when(jnp.logical_and(zt >= z, has_below))
+        def _():
+            gather(1, t, c, below).wait_send()
+
     def finish(zt, _):
-        def one(c, _):
-            @pl.when(jnp.logical_and(zt <= z, has_above))
-            def _():
-                gather(0, zt, c, above).wait_send()
-
-            @pl.when(jnp.logical_and(zt >= z, has_below))
-            def _():
-                gather(1, zt, c, below).wait_send()
-
-            gather(2, zt, c, partner).wait_send()
-            x_sum(zt, c).wait_send()
+        t = zt * COLUMNS + x
+        sent(zt, zt * COLUMNS + (1 - x), me_e)
+
+        @pl.when(zt != z)
+        def _():
+            cross_sum(0, zt, partner).wait_send()
+
+        def one(i, _):
+            c = lax.rem(me_e + i, groups)
+            sent(zt, t, c)
+
+            @pl.when(jnp.logical_or(zt == z, i > 0))
+            def _():
+                gather(2, t, c, partner).wait_send()
+                x_sum(zt, c).wait_send()
 
             @pl.when(zt != z)
             def _():
@@ -300,15 +356,18 @@
             pltpu.VMEM((tp,) + chunk, kind),
             pltpu.VMEM((depth,) + chunk, kind),
             pltpu.VMEM((2, depth) + chunk, kind),
+            pltpu.VMEM((2, depth) + chunk[1:], kind),
             pltpu.VMEM(chunk, kind),
             dma((3,)),
             dma((groups,)),
-            dma((3, depth, groups)),
+            dma((3, tp, groups)),
             dma((tp, groups)),
             dma((depth, groups)),
             dma((depth, groups)),
             dma((depth, groups)),
             dma((2, depth, groups)),
+            dma((depth,)),
+            dma((2, depth)),
             dma((groups,)),
             dma((groups,)),
         ],

time: 207 us -> 228 us (1.10)
  Pallas kernels: 200 us -> 219 us
    pallas_call x1, Pallas kernels: 176 us -> 195 us  [expert_exchange(): pl.pallas_call(functools.partial(expert_kernel, groups, depth, capacity),...]
where the time goes in v3:
time: 228 us; the launch traced here: 227 us
  Pallas kernels  219 us (96%)
  matrix products  3.01 us (1%)
  local copies, waits for them, and re-layouts  2.86 us (1%)
    pallas_call x1, Pallas kernels, expert_exchange(): pl.pallas_call(functools.partial(expert_kernel, groups, depth, capacity),...  195 us
    pallas_call x1, Pallas kernels, attention_exchange(): pl.pallas_call(functools.partial(attention_kernel, groups, sites), out_sh...  23.9 us

profile of v3, /device:TPU:13, one launch (start us, length us, event | category | flops | bytes accessed | tf_op | source)
XLA Modules:
  0.0 226.6 jit_solution(16369520341322152052)
XLA Ops:
  0.0 0.0 copy-start
  0.0 1.5 copy.12
  1.5 0.0 copy-start.2
  1.5 23.9 %shard_map.91 = bf16[4,32,1792]{2,1,0:T(8,128)(2,1)S(1)} custom-call(bf16[4,96,1792]{2,1,0:T(8,128)(2,1)S(1)} %bitcast.35), custom_call_target="tpu_custom_call" | custom-call | flops 234881024 | bytes 2064384 | tf_op jit(solution)/shard_map/pallas_call | solution.py:513
  25.4 0.0 copy-done
  25.4 0.0 copy-start.1
  25.4 0.0 copy-start.3
  25.5 0.2 multiply_reduce_fusion
  25.7 0.1 rsqrt.12
  25.8 0.0 copy-done.2
  25.8 0.1 fusion.1
  25.9 0.2 copy-done.1
  26.1 0.0 copy-done.3
  26.2 0.1 select_n.21
  26.2 0.1 fusion.2
  26.4 1.4 convolution_convert_fusion
  27.7 195.3 %shard_map.92 = bf16[4,64,1792]{2,1,0:T(8,128)(2,1)} custom-call(bf16[4,64,1792]{2,1,0:T(8,128)(2,1)} %bitcast.39, bf16[2,1792,896]{2,1,0:T(8,128)(2,1)} %wg_hbm.1, bf16[2,1792,896]{2,1,0:T(8,128)(2,1)} %wu_hbm.1, bf16[2,896,1792]{2,1,0:T(8,128)(2,1)} %wd_hbm.1), custom_call_target="tpu_custom_call" | custom-call | flops 19730006016 | bytes 19267584 | tf_op jit(solution)/shard_map/pallas_call | solution.py:345
  223.0 1.6 convolution_bitcast_fusion
  224.6 0.0 copy-start.4
  224.6 0.1 fusion.4
  224.8 0.5 copy-done.4
  225.3 0.1 select_n.19
  225.4 0.1 mul.53
  225.5 0.1 mul.63
  225.6 1.0 add_convert_fusion
  (6 shorter events, 0.1 us)
Async XLA Ops:
  0.0 25.4 %copy-start = (bf16[4,32,1792]{2,1,0:T(8,128)(2,1)S(1)}, bf16[4,32,1792]{2,1,0:T(8,128)(2,1)}, u32[]{:S(2)}) copy-start(bf16[4,32,1792]{2,1,0:T(8,128)(2,1)} %param.10) | copy-start | bytes 1376260
  1.5 24.3 %copy-start.2 = (f32[1792]{0:T(1024)S(1)}, f32[1792]{0:T(1024)}, u32[]{:S(2)}) copy-start(f32[1792]{0:T(1024)} %param.11) | copy-start | bytes 21508
  25.4 0.7 copy-start.1
  25.4 0.7 copy-start.3
  224.6 0.7 copy-start.4

commit v4 on v2

--- a/solution.py
+++ b/solution.py
@@ -44,7 +44,7 @@
     experts = wg.shape[0]
     width = rows.shape[-1]
     order = near_first(depth)
-    sums = [[row[-2], row[-1]] + row[-3::-1] for row in order]
+    sums = [row[::-1] for row in order]
 
     weight_copies = [
         pltpu.make_async_copy(src, dst, w_sem.at[i])
@@ -170,10 +170,6 @@
             for copy in weight_copies:
                 copy.wait()
 
-        @pl.when(it == depth)
-        def _():
-            start_x(0, 0)
-
         def side(h, _):
             at = it - h
 
@@ -199,7 +195,7 @@
 
     lax.fori_loop(0, depth + 1, stage, 0)
 
-    lax.fori_loop(1, depth, start_x, 0)
+    lax.fori_loop(0, depth, start_x, 0)
 
     def reduce_target(k, _):
         zt = lookup(sums, z, k)

time: 207 us -> 202 us (0.976)
  Pallas kernels: 200 us -> 194 us
    pallas_call x1, Pallas kernels: 176 us -> 170 us  [expert_exchange(): pl.pallas_call(functools.partial(expert_kernel, groups, depth, capacity),...]
where the time goes in v4:
time: 202 us; the launch traced here: 201 us
  Pallas kernels  194 us (96%)
  matrix products  3.01 us (1%)
  local copies, waits for them, and re-layouts  2.86 us (1%)
    pallas_call x1, Pallas kernels, expert_exchange(): pl.pallas_call(functools.partial(expert_kernel, groups, depth, capacity),...  170 us
    pallas_call x1, Pallas kernels, attention_exchange(): pl.pallas_call(functools.partial(attention_kernel, groups, sites), out_sh...  23.9 us

profile of v4, /device:TPU:13, one launch (start us, length us, event | category | flops | bytes accessed | tf_op | source)
XLA Modules:
  0.0 201.2 jit_solution(10884021541065295662)
XLA Ops:
  0.0 0.0 copy-start
  0.0 1.5 copy.12
  1.5 0.0 copy-start.2
  1.5 23.9 %shard_map.91 = bf16[4,32,1792]{2,1,0:T(8,128)(2,1)S(1)} custom-call(bf16[4,96,1792]{2,1,0:T(8,128)(2,1)S(1)} %bitcast.35), custom_call_target="tpu_custom_call" | custom-call | flops 234881024 | bytes 2064384 | tf_op jit(solution)/shard_map/pallas_call | solution.py:450
  25.4 0.0 copy-done
  25.4 0.0 copy-start.1
  25.4 0.0 copy-start.3
  25.5 0.2 multiply_reduce_fusion
  25.7 0.1 rsqrt.12
  25.8 0.0 copy-done.2
  25.8 0.1 fusion.1
  25.9 0.2 copy-done.1
  26.1 0.0 copy-done.3
  26.2 0.1 select_n.21
  26.2 0.1 fusion.2
  26.4 1.4 convolution_convert_fusion
  27.7 169.9 %shard_map.92 = bf16[4,64,1792]{2,1,0:T(8,128)(2,1)} custom-call(bf16[4,64,1792]{2,1,0:T(8,128)(2,1)} %bitcast.39, bf16[2,1792,896]{2,1,0:T(8,128)(2,1)} %wg_hbm.1, bf16[2,1792,896]{2,1,0:T(8,128)(2,1)} %wu_hbm.1, bf16[2,896,1792]{2,1,0:T(8,128)(2,1)} %wd_hbm.1), custom_call_target="tpu_custom_call" | custom-call | flops 19730006016 | bytes 19267584 | tf_op jit(solution)/shard_map/pallas_call | solution.py:285
  197.6 1.6 convolution_bitcast_fusion
  199.2 0.0 copy-start.4
  199.3 0.1 fusion.4
  199.4 0.5 copy-done.4
  199.9 0.1 select_n.19
  200.1 0.1 mul.53
  200.1 0.1 mul.63
  200.2 1.0 add_convert_fusion
  (6 shorter events, 0.1 us)
Async XLA Ops:
  0.0 25.4 %copy-start = (bf16[4,32,1792]{2,1,0:T(8,128)(2,1)S(1)}, bf16[4,32,1792]{2,1,0:T(8,128)(2,1)}, u32[]{:S(2)}) copy-start(bf16[4,32,1792]{2,1,0:T(8,128)(2,1)} %param.10) | copy-start | bytes 1376260
  1.5 24.3 %copy-start.2 = (f32[1792]{0:T(1024)S(1)}, f32[1792]{0:T(1024)}, u32[]{:S(2)}) copy-start(f32[1792]{0:T(1024)} %param.11) | copy-start | bytes 21508
  25.4 0.7 copy-start.1
  25.4 0.7 copy-start.3
  199.2 0.7 copy-start.4
